TPU v7x, 32 devices: a whole 2x2x4 slice. The times are simulated.
32 devices in a mesh: blk: 8 (over z, y), head: 4 (over x, core).
Axes of the slice: x: 2, y: 2, z: 4, core: 2. Of those that a mesh axis runs over, the one named last changes fastest.
Arguments:
- query_heads: bfloat16 [1536, 24576], P('blk', 'head'), may hold values from -200 to 200
- latent_cache: bfloat16 [1536, 512], P('blk'), may hold values from -6 to 6
- rope_keys: bfloat16 [1536, 64], P('blk'), may hold values from -10 to 10
- up_weight: bfloat16 [512, 32768], P('blk', 'head'), may hold values from -0.25 to 0.25
- out_weight: bfloat16 [16384, 5120], P('head'), may hold values from -0.046875 to 0.046875
- block_mask: int32 [16, 16], replicated, may hold values from 0 to 1, as said below
Outputs:
- attended: bfloat16 [1536, 5120], P('blk', 'head')
Inputs may be any that keep to these rules, and one draw needn't show every extreme that they name: block_mask[i, i] is 1 and block_mask[i, j] is 0 for j > i; entries below the diagonal are 0 or 1.
All inputs are finite; a program needn't handle non-finite values.
Results may differ from a plain program's by a relative error of at most 0.019.
Values may be sent and summed in bfloat16 or wider, within the bound.
A program may use at most 128 MiB of HBM per device.

v0:
```python
import math

import jax
import jax.numpy as jnp
from jax import lax
from jax.sharding import PartitionSpec as P

DN = 128
DR = 64
DV = 128
QB = 96


NEG_FILL = -1e30


def from_behind(value, axis, steps):
    count = lax.axis_size(axis)
    initial, last = (max(0, -steps), min(count, count - steps))
    return lax.ppermute(value, axis, [(source, source + steps) for source in range(initial, last)])


def advance(payload):
    return from_behind((payload[0], payload[1]), "blk", 1)


def per_device(query_heads, latent_cache, rope_keys, up_weight, out_weight, block_mask):
    tok_rows = query_heads.shape[0]
    head_count = out_weight.shape[0] // DV
    cycle_size = lax.axis_size("blk")
    my_index = lax.axis_index("blk")
    groups = tok_rows // QB
    queries = query_heads.reshape(tok_rows, head_count, DN + DR)
    starts = [my_index * tok_rows + group_index * QB for group_index in range(groups)]
    query_nope = queries[:, :, :DN]
    query_rot = queries[:, :, DN:]
    full_up = lax.all_gather(up_weight, "blk", axis=0, tiled=True)
    score_scale = 1.0 / math.sqrt(DN + DR)

    def key_values(carried_block):
        return jnp.dot(carried_block, full_up, preferred_element_type=jnp.float32).astype(
            jnp.bfloat16
        )

    payload = (latent_cache, rope_keys)

    def allowed_for(source):
        key_position = source * tok_rows + jnp.arange(tok_rows, dtype=jnp.int32)
        first_block = source * groups
        pieces = []
        for group_index in range(groups):
            block_row = starts[group_index] // QB
            row_bits = lax.dynamic_slice(block_mask, (block_row, first_block), (1, groups))
            key_bits = jnp.repeat(row_bits[0], QB) == 1
            query_position = starts[group_index] + jnp.arange(QB, dtype=jnp.int32)
            pieces.append(key_bits[None, :] & (key_position[None, :] <= query_position[:, None]))
        return jnp.concatenate(pieces, axis=0)

    def attend(status, payload, source):
        allowed = allowed_for(source)

        def update(carried):
            running_max, denominator, summed = carried
            expanded = key_values(payload[0]).reshape(tok_rows, head_count, DN + DV)
            scores = jnp.einsum(
                "qhd,khd->hqk", query_nope, expanded[:, :, :DN], preferred_element_type=jnp.float32
            )
            scores = scores + jnp.einsum(
                "qhr,kr->hqk", query_rot, payload[1], preferred_element_type=jnp.float32
            )
            scores = jnp.where(allowed[None], scores * score_scale, NEG_FILL)
            newest = jnp.maximum(running_max, jnp.max(scores, axis=2))
            factor = jnp.exp(running_max - newest)
            weights = jnp.where(allowed[None], jnp.exp(scores - newest[:, :, None]), 0.0)
            denominator = denominator * factor + jnp.sum(weights, axis=2)
            summed = summed * factor[:, :, None] + jnp.einsum(
                "hqk,khv->hqv",
                weights.astype(jnp.bfloat16),
                expanded[:, :, DN:],
                preferred_element_type=jnp.float32,
            )
            return (newest, denominator, summed)

        return lax.cond(jnp.any(allowed), update, lambda carried: carried, status)

    status = (
        jnp.full((head_count, tok_rows), NEG_FILL, jnp.float32),
        jnp.zeros((head_count, tok_rows), jnp.float32),
        jnp.zeros((head_count, tok_rows, DV), jnp.float32),
    )
    status = attend(status, payload, my_index)

    def cycle_turn(turn_index, carried):
        moving, current = carried
        moving = advance(moving)
        source = (my_index - turn_index) % cycle_size
        return (moving, attend(current, moving, source))

    payload, status = lax.fori_loop(1, cycle_size, cycle_turn, (payload, status))
    running_max, denominator, summed = status
    outputs = (summed / denominator[:, :, None]).astype(jnp.bfloat16)
    outputs = jnp.transpose(outputs, (1, 0, 2)).reshape(tok_rows, head_count * DV)
    partial_sum = jnp.dot(outputs, out_weight, preferred_element_type=jnp.float32)
    return lax.psum_scatter(
        partial_sum.astype(jnp.bfloat16), "head", scatter_dimension=1, tiled=True
    )


def solution(mesh):
    return jax.shard_map(
        per_device,
        mesh=mesh,
        in_specs=(
            P("blk", "head"),
            P("blk", None),
            P("blk", None),
            P("blk", "head"),
            P("head", None),
            P(),
        ),
        out_specs=P("blk", "head"),
        check_vma=False,
    )
```

profile of v0, /device:TPU:24, one launch (start us, length us, event | category | flops | bytes accessed | tf_op | source)
XLA Modules:
  0.0 395.6 jit_solution(13821440536448981145)
XLA Ops:
  6.5 1.6 copy.80
  9.0 4.5 %copy.22 = bf16[192,6144]{0,1:T(8,128)(2,1)} copy(bf16[192,6144]{1,0:T(8,128)(2,1)} %param.12) | data formatting | bytes 4718592 | tf_op args[0]
  13.6 1.7 slice.24
  15.3 2.3 slice.25
  20.8 2.8 copy.24
  23.7 109.8 %all-gather.2.cloned.1.call-done = bf16[512,8192]{1,0:T(8,128)(2,1)} async-done(((bf16[64,8192]{1,0:T(8,128)(2,1)}), bf16[512,8192]{1,0:T(8,128)(2,1)}) %all-gather.2.cloned.1.call-update) | async-done | bytes 8388624 | tf_op jit(solution)/shard_map/all_gather | solution.py:37
  133.5 17.0 %conditional.2 = (f32[32,192]{1,0:T(8,128)}, f32[32,192]{1,0:T(8,128)S(1)}, f32[32,192,128]{2,1,0:T(8,128)S(1)}) conditional(s32[]{:T(128)} %convert_element_type.32, () %tuple.45, (pred[192,192]{0,1:T(8,128)(4,1)S(1)}, bf16[192,512]{1,0:T(8,128)(2,1)}, bf16[512,8192]{1,0:T(8,128)(2,1)}, bf16[192,32,128]{0,2,1:T(8,128)(2,1)S(1)}, ...), branch_computations={%region_2.3_spmd, %region_3.0_spmd} | conditional | flops 2379767808 | bytes 60108852 | solution.py:84
  133.5 5.3 %convolution_convert_fusion = bf16[192,8192]{1,0:T(8,128)(2,1)S(1)} fusion(bf16[192,512]{1,0:T(8,128)(2,1)} %get-tuple-element.468, bf16[512,8192]{1,0:T(8,128)(2,1)} %get-tuple-element.469), kind=kOutput, calls=%fused_computation | convolution fusion | flops 1612185600 | bytes 11730944 | tf_op jit(solution)/shard_map/cond/branch_1_fun/dot_general | solution.py:41
  141.5 1.8 fusion.42
  144.0 2.0 fusion.3
  146.7 3.6 fusion.9
  150.5 174.1 %while.24 = (s32[]{:T(128)}, bf16[192,512]{1,0:T(8,128)(2,1)}, bf16[192,64]{0,1:T(8,128)(2,1)S(1)}, f32[32,192]{1,0:T(8,128)}, f32[32,192]{1,0:T(8,128)S(1)}, /*...) while((s32[]{:T(128)}, bf16[192,512]{1,0:T(8,128)(2,1)}, ...), condition=%wide.region_13.14_spmd, body=%wide.region_6.13_spmd.sunk | while | flops 2380689920 | bytes 71111864 | solution.py:99
  150.5 2.4 collective-permute-start
  152.9 1.9 collective-permute-start.1
  158.1 3.0 collective-permute-done.1
  161.1 17.5 %conditional.4 = ((f32[32,192]{1,0:T(8,128)}, f32[32,192]{1,0:T(8,128)S(1)}, f32[32,192,128]{2,1,0:T(8,128)S(1)})) conditional(s32[]{:T(128)} %convert_element_type.52, (f32[32,192]{1,0:T(8,128)}, f32[32,192]{1,0:T(8,128)S(1)}, f32[32,192,128]{2,1,0:T(8,128)S(1)}) %tuple.84, (pred[192,192]{0,1:T(8,128)(4,1)S(1)}, bf16[192,512]{1,0:T(8,128)(2,1)S(1)}, ...), branch_computations={%region_9.9_spmd, %region_10.12_spmd} | conditional | flops 2380541952 | bytes 69668952 | solution.py:84
  161.1 5.2 %convolution_convert_fusion.1 = bf16[192,8192]{1,0:T(8,128)(2,1)S(1)} fusion(bf16[192,512]{1,0:T(8,128)(2,1)S(1)} %get-tuple-element.475, bf16[512,8192]{1,0:T(8,128)(2,1)} %get-tuple-element.476), kind=kOutput, calls=%fused_computation.20 | convolution fusion | flops 1612185600 | bytes 11730944 | tf_op jit(solution)/shard_map/while/body/eval_jaxpr/cond/branch_1_fun/dot_general | solution.py:41
  168.6 1.0 fusion.30
  169.8 1.8 fusion.44
  172.4 1.3 fusion.21
  174.5 3.5 multiply_add_fusion
  179.3 1.9 collective-permute-start
  181.2 1.9 collective-permute-start.1
  186.4 2.6 collective-permute-done.1
  189.0 17.5 %conditional.4 = ((f32[32,192]{1,0:T(8,128)}, f32[32,192]{1,0:T(8,128)S(1)}, f32[32,192,128]{2,1,0:T(8,128)S(1)})) conditional(s32[]{:T(128)} %convert_element_type.52, (f32[32,192]{1,0:T(8,128)}, f32[32,192]{1,0:T(8,128)S(1)}, f32[32,192,128]{2,1,0:T(8,128)S(1)}) %tuple.84, (pred[192,192]{0,1:T(8,128)(4,1)S(1)}, bf16[192,512]{1,0:T(8,128)(2,1)S(1)}, ...), branch_computations={%region_9.9_spmd, %region_10.12_spmd} | conditional | flops 2380541952 | bytes 69668952 | solution.py:84
  189.0 5.2 %convolution_convert_fusion.1 = bf16[192,8192]{1,0:T(8,128)(2,1)S(1)} fusion(bf16[192,512]{1,0:T(8,128)(2,1)S(1)} %get-tuple-element.475, bf16[512,8192]{1,0:T(8,128)(2,1)} %get-tuple-element.476), kind=kOutput, calls=%fused_computation.20 | convolution fusion | flops 1612185600 | bytes 11730944 | tf_op jit(solution)/shard_map/while/body/eval_jaxpr/cond/branch_1_fun/dot_general | solution.py:41
  196.5 1.0 fusion.30
  197.7 1.8 fusion.44
  200.3 1.3 fusion.21
  202.4 3.5 multiply_add_fusion
  207.2 1.9 collective-permute-start
  209.1 1.9 collective-permute-start.1
  214.3 1.9 collective-permute-done.1
  216.9 18.6 %collective-permute-start = (bf16[192,512]{1,0:T(8,128)(2,1)}, bf16[192,512]{1,0:T(8,128)(2,1)S(1)}, u32[]{:S(2)}, u32[]{:S(2)}) collective-permute-start(bf16[192,512]{1,0:T(8,128)(2,1)} %get-tuple-element.759), channel_id=1, source_target_pairs={{0,4},{4,8},{8,12},{12,16},{16,20},{20,24},{24,28},{1,5},{5,9},{9,... | collective-permute-start | bytes 589832 | tf_op jit(solution)/shard_map/while/body/eval_jaxpr/ppermute | solution.py:20
  235.5 1.9 collective-permute-start.1
  240.7 1.5 collective-permute-done.1
  242.2 17.5 %conditional.4 = ((f32[32,192]{1,0:T(8,128)}, f32[32,192]{1,0:T(8,128)S(1)}, f32[32,192,128]{2,1,0:T(8,128)S(1)})) conditional(s32[]{:T(128)} %convert_element_type.52, (f32[32,192]{1,0:T(8,128)}, f32[32,192]{1,0:T(8,128)S(1)}, f32[32,192,128]{2,1,0:T(8,128)S(1)}) %tuple.84, (pred[192,192]{0,1:T(8,128)(4,1)S(1)}, bf16[192,512]{1,0:T(8,128)(2,1)S(1)}, ...), branch_computations={%region_9.9_spmd, %region_10.12_spmd} | conditional | flops 2380541952 | bytes 69668952 | solution.py:84
  242.2 5.2 %convolution_convert_fusion.1 = bf16[192,8192]{1,0:T(8,128)(2,1)S(1)} fusion(bf16[192,512]{1,0:T(8,128)(2,1)S(1)} %get-tuple-element.475, bf16[512,8192]{1,0:T(8,128)(2,1)} %get-tuple-element.476), kind=kOutput, calls=%fused_computation.20 | convolution fusion | flops 1612185600 | bytes 11730944 | tf_op jit(solution)/shard_map/while/body/eval_jaxpr/cond/branch_1_fun/dot_general | solution.py:41
  249.7 1.0 fusion.30
  251.0 1.8 fusion.44
  253.5 1.3 fusion.21
  255.6 3.5 multiply_add_fusion
  260.4 1.9 collective-permute-start
  262.3 1.9 collective-permute-start.1
  267.5 1.9 collective-permute-done.1
  269.4 17.5 %conditional.4 = ((f32[32,192]{1,0:T(8,128)}, f32[32,192]{1,0:T(8,128)S(1)}, f32[32,192,128]{2,1,0:T(8,128)S(1)})) conditional(s32[]{:T(128)} %convert_element_type.52, (f32[32,192]{1,0:T(8,128)}, f32[32,192]{1,0:T(8,128)S(1)}, f32[32,192,128]{2,1,0:T(8,128)S(1)}) %tuple.84, (pred[192,192]{0,1:T(8,128)(4,1)S(1)}, bf16[192,512]{1,0:T(8,128)(2,1)S(1)}, ...), branch_computations={%region_9.9_spmd, %region_10.12_spmd} | conditional | flops 2380541952 | bytes 69668952 | solution.py:84
  269.4 5.2 %convolution_convert_fusion.1 = bf16[192,8192]{1,0:T(8,128)(2,1)S(1)} fusion(bf16[192,512]{1,0:T(8,128)(2,1)S(1)} %get-tuple-element.475, bf16[512,8192]{1,0:T(8,128)(2,1)} %get-tuple-element.476), kind=kOutput, calls=%fused_computation.20 | convolution fusion | flops 1612185600 | bytes 11730944 | tf_op jit(solution)/shard_map/while/body/eval_jaxpr/cond/branch_1_fun/dot_general | solution.py:41
  277.0 1.0 fusion.30
  278.2 1.8 fusion.44
  280.7 1.3 fusion.21
  282.8 3.5 multiply_add_fusion
  287.6 1.9 collective-permute-start
  289.5 1.9 collective-permute-start.1
  294.7 1.9 collective-permute-done.1
  296.6 17.5 %conditional.4 = ((f32[32,192]{1,0:T(8,128)}, f32[32,192]{1,0:T(8,128)S(1)}, f32[32,192,128]{2,1,0:T(8,128)S(1)})) conditional(s32[]{:T(128)} %convert_element_type.52, (f32[32,192]{1,0:T(8,128)}, f32[32,192]{1,0:T(8,128)S(1)}, f32[32,192,128]{2,1,0:T(8,128)S(1)}) %tuple.84, (pred[192,192]{0,1:T(8,128)(4,1)S(1)}, bf16[192,512]{1,0:T(8,128)(2,1)S(1)}, ...), branch_computations={%region_9.9_spmd, %region_10.12_spmd} | conditional | flops 2380541952 | bytes 69668952 | solution.py:84
  296.6 5.2 %convolution_convert_fusion.1 = bf16[192,8192]{1,0:T(8,128)(2,1)S(1)} fusion(bf16[192,512]{1,0:T(8,128)(2,1)S(1)} %get-tuple-element.475, bf16[512,8192]{1,0:T(8,128)(2,1)} %get-tuple-element.476), kind=kOutput, calls=%fused_computation.20 | convolution fusion | flops 1612185600 | bytes 11730944 | tf_op jit(solution)/shard_map/while/body/eval_jaxpr/cond/branch_1_fun/dot_general | solution.py:41
  305.4 1.8 fusion.44
  308.0 1.3 fusion.21
  310.0 3.5 multiply_add_fusion
  314.8 1.9 collective-permute-start
  316.7 1.9 collective-permute-start.1
  322.0 1.9 collective-permute-done.1
  324.5 17.3 %convolution_convert_fusion.2 = bf16[192,5120]{1,0:T(8,128)(2,1)} fusion(bf16[4096,5120]{1,0:T(8,128)(2,1)} %param.16, f32[32,192,128]{2,1,0:T(8,128)S(1)} %get-tuple-element.509, f32[32,192]{1,0:T(8,128)S(1)} %get-tuple-element.510), kind=kOutput, calls=%fused_computation.49 | convolution fusion | flops 8055619584 | bytes 47079424 | tf_op jit(solution)/shard_map/dot_general | solution.py:103
  341.9 46.9 %reduce-scatter.2.cloned.1.call-done = bf16[192,1280]{1,0:T(8,128)(2,1)} async-done(((bf16[192,5120]{1,0:T(8,128)(2,1)}), bf16[192,1280]{1,0:T(8,128)(2,1)}) %reduce-scatter.2.cloned.1.call-update) | async-done | bytes 491536 | tf_op jit(solution)/shard_map/reduce_scatter | solution.py:104
  (153 shorter events, 50.8 us)
Async XLA Ops:
  6.5 127.0 %all-gather.2.cloned.1.call-start = ((), (), s32[]{:S(2)}) async-start(), calls=%async_computation.1 | async-start | bytes 9437184 | tf_op jit(solution)/shard_map/all_gather | solution.py:37
  8.9 379.9 %reduce-scatter.2.cloned.1.call-start = ((), (), s32[]{:S(2)}) async-start(), calls=%async_computation.2 | async-start | bytes 2457600 | tf_op jit(solution)/shard_map/reduce_scatter | solution.py:104
  140.3 1.2 copy-start.1
  150.5 10.6 %collective-permute-start = (bf16[192,512]{1,0:T(8,128)(2,1)}, bf16[192,512]{1,0:T(8,128)(2,1)S(1)}, u32[]{:S(2)}, u32[]{:S(2)}) collective-permute-start(bf16[192,512]{1,0:T(8,128)(2,1)} %get-tuple-element.759), channel_id=1, source_target_pairs={{0,4},{4,8},{8,12},{12,16},{16,20},{20,24},{24,28},{1,5},{5,9},{9,... | collective-permute-start | bytes 589832 | tf_op jit(solution)/shard_map/while/body/eval_jaxpr/ppermute | solution.py:20
  152.9 8.2 %collective-permute-start.1 = (bf16[192,64]{0,1:T(8,128)(2,1)S(1)}, bf16[192,64]{0,1:T(8,128)(2,1)S(1)}, u32[]{:S(2)}, u32[]{:S(2)}) collective-permute-start(bf16[192,64]{0,1:T(8,128)(2,1)S(1)} %get-tuple-element.760), channel_id=1, source_target_pairs={{0,4},{4,8},{8,12},{12,16},{16,20},{20,24},{24,28},{1,5},{5,9},{9,... | collective-permute-start | bytes 73736 | tf_op jit(solution)/shard_map/while/body/eval_jaxpr/ppermute | solution.py:20
  167.2 1.4 copy-start
  168.6 1.2 copy-start.2
  179.3 9.7 %collective-permute-start = (bf16[192,512]{1,0:T(8,128)(2,1)}, bf16[192,512]{1,0:T(8,128)(2,1)S(1)}, u32[]{:S(2)}, u32[]{:S(2)}) collective-permute-start(bf16[192,512]{1,0:T(8,128)(2,1)} %get-tuple-element.759), channel_id=1, source_target_pairs={{0,4},{4,8},{8,12},{12,16},{16,20},{20,24},{24,28},{1,5},{5,9},{9,... | collective-permute-start | bytes 589832 | tf_op jit(solution)/shard_map/while/body/eval_jaxpr/ppermute | solution.py:20
  181.2 7.8 %collective-permute-start.1 = (bf16[192,64]{0,1:T(8,128)(2,1)S(1)}, bf16[192,64]{0,1:T(8,128)(2,1)S(1)}, u32[]{:S(2)}, u32[]{:S(2)}) collective-permute-start(bf16[192,64]{0,1:T(8,128)(2,1)S(1)} %get-tuple-element.760), channel_id=1, source_target_pairs={{0,4},{4,8},{8,12},{12,16},{16,20},{20,24},{24,28},{1,5},{5,9},{9,... | collective-permute-start | bytes 73736 | tf_op jit(solution)/shard_map/while/body/eval_jaxpr/ppermute | solution.py:20
  195.1 1.4 copy-start
  196.5 1.2 copy-start.2
  207.2 9.0 %collective-permute-start = (bf16[192,512]{1,0:T(8,128)(2,1)}, bf16[192,512]{1,0:T(8,128)(2,1)S(1)}, u32[]{:S(2)}, u32[]{:S(2)}) collective-permute-start(bf16[192,512]{1,0:T(8,128)(2,1)} %get-tuple-element.759), channel_id=1, source_target_pairs={{0,4},{4,8},{8,12},{12,16},{16,20},{20,24},{24,28},{1,5},{5,9},{9,... | collective-permute-start | bytes 589832 | tf_op jit(solution)/shard_map/while/body/eval_jaxpr/ppermute | solution.py:20
  209.1 7.1 %collective-permute-start.1 = (bf16[192,64]{0,1:T(8,128)(2,1)S(1)}, bf16[192,64]{0,1:T(8,128)(2,1)S(1)}, u32[]{:S(2)}, u32[]{:S(2)}) collective-permute-start(bf16[192,64]{0,1:T(8,128)(2,1)S(1)} %get-tuple-element.760), channel_id=1, source_target_pairs={{0,4},{4,8},{8,12},{12,16},{16,20},{20,24},{24,28},{1,5},{5,9},{9,... | collective-permute-start | bytes 73736 | tf_op jit(solution)/shard_map/while/body/eval_jaxpr/ppermute | solution.py:20
  216.9 25.3 %collective-permute-start = (bf16[192,512]{1,0:T(8,128)(2,1)}, bf16[192,512]{1,0:T(8,128)(2,1)S(1)}, u32[]{:S(2)}, u32[]{:S(2)}) collective-permute-start(bf16[192,512]{1,0:T(8,128)(2,1)} %get-tuple-element.759), channel_id=1, source_target_pairs={{0,4},{4,8},{8,12},{12,16},{16,20},{20,24},{24,28},{1,5},{5,9},{9,... | collective-permute-start | bytes 589832 | tf_op jit(solution)/shard_map/while/body/eval_jaxpr/ppermute | solution.py:20
  235.5 6.7 %collective-permute-start.1 = (bf16[192,64]{0,1:T(8,128)(2,1)S(1)}, bf16[192,64]{0,1:T(8,128)(2,1)S(1)}, u32[]{:S(2)}, u32[]{:S(2)}) collective-permute-start(bf16[192,64]{0,1:T(8,128)(2,1)S(1)} %get-tuple-element.760), channel_id=1, source_target_pairs={{0,4},{4,8},{8,12},{12,16},{16,20},{20,24},{24,28},{1,5},{5,9},{9,... | collective-permute-start | bytes 73736 | tf_op jit(solution)/shard_map/while/body/eval_jaxpr/ppermute | solution.py:20
  248.3 1.4 copy-start
  249.7 1.2 copy-start.2
  260.4 9.0 %collective-permute-start = (bf16[192,512]{1,0:T(8,128)(2,1)}, bf16[192,512]{1,0:T(8,128)(2,1)S(1)}, u32[]{:S(2)}, u32[]{:S(2)}) collective-permute-start(bf16[192,512]{1,0:T(8,128)(2,1)} %get-tuple-element.759), channel_id=1, source_target_pairs={{0,4},{4,8},{8,12},{12,16},{16,20},{20,24},{24,28},{1,5},{5,9},{9,... | collective-permute-start | bytes 589832 | tf_op jit(solution)/shard_map/while/body/eval_jaxpr/ppermute | solution.py:20
  262.3 7.1 %collective-permute-start.1 = (bf16[192,64]{0,1:T(8,128)(2,1)S(1)}, bf16[192,64]{0,1:T(8,128)(2,1)S(1)}, u32[]{:S(2)}, u32[]{:S(2)}) collective-permute-start(bf16[192,64]{0,1:T(8,128)(2,1)S(1)} %get-tuple-element.760), channel_id=1, source_target_pairs={{0,4},{4,8},{8,12},{12,16},{16,20},{20,24},{24,28},{1,5},{5,9},{9,... | collective-permute-start | bytes 73736 | tf_op jit(solution)/shard_map/while/body/eval_jaxpr/ppermute | solution.py:20
  275.5 1.4 copy-start
  277.0 1.2 copy-start.2
  287.6 9.0 %collective-permute-start = (bf16[192,512]{1,0:T(8,128)(2,1)}, bf16[192,512]{1,0:T(8,128)(2,1)S(1)}, u32[]{:S(2)}, u32[]{:S(2)}) collective-permute-start(bf16[192,512]{1,0:T(8,128)(2,1)} %get-tuple-element.759), channel_id=1, source_target_pairs={{0,4},{4,8},{8,12},{12,16},{16,20},{20,24},{24,28},{1,5},{5,9},{9,... | collective-permute-start | bytes 589832 | tf_op jit(solution)/shard_map/while/body/eval_jaxpr/ppermute | solution.py:20
  289.5 7.1 %collective-permute-start.1 = (bf16[192,64]{0,1:T(8,128)(2,1)S(1)}, bf16[192,64]{0,1:T(8,128)(2,1)S(1)}, u32[]{:S(2)}, u32[]{:S(2)}) collective-permute-start(bf16[192,64]{0,1:T(8,128)(2,1)S(1)} %get-tuple-element.760), channel_id=1, source_target_pairs={{0,4},{4,8},{8,12},{12,16},{16,20},{20,24},{24,28},{1,5},{5,9},{9,... | collective-permute-start | bytes 73736 | tf_op jit(solution)/shard_map/while/body/eval_jaxpr/ppermute | solution.py:20
  302.8 1.4 copy-start
  304.2 1.2 copy-start.2
  314.8 9.0 %collective-permute-start = (bf16[192,512]{1,0:T(8,128)(2,1)}, bf16[192,512]{1,0:T(8,128)(2,1)S(1)}, u32[]{:S(2)}, u32[]{:S(2)}) collective-permute-start(bf16[192,512]{1,0:T(8,128)(2,1)} %get-tuple-element.759), channel_id=1, source_target_pairs={{0,4},{4,8},{8,12},{12,16},{16,20},{20,24},{24,28},{1,5},{5,9},{9,... | collective-permute-start | bytes 589832 | tf_op jit(solution)/shard_map/while/body/eval_jaxpr/ppermute | solution.py:20
  316.7 7.1 %collective-permute-start.1 = (bf16[192,64]{0,1:T(8,128)(2,1)S(1)}, bf16[192,64]{0,1:T(8,128)(2,1)S(1)}, u32[]{:S(2)}, u32[]{:S(2)}) collective-permute-start(bf16[192,64]{0,1:T(8,128)(2,1)S(1)} %get-tuple-element.760), channel_id=1, source_target_pairs={{0,4},{4,8},{8,12},{12,16},{16,20},{20,24},{24,28},{1,5},{5,9},{9,... | collective-permute-start | bytes 73736 | tf_op jit(solution)/shard_map/while/body/eval_jaxpr/ppermute | solution.py:20
Sparse Core Ops, SparseCore 0:
  9.5 123.9 all-gather.1
  342.0 46.7 reduce-scatter.1
where the time goes:
time: 401 us; the launch traced here: 396 us
  waiting for transfers between devices  171 us (43%)
  matrix products  86.5 us (22%)
  starting transfers between devices  44 us (11%)
  local copies, waits for them, and re-layouts  38.5 us (10%)
  other arithmetic  31.5 us (8%)
  between operations  14.6 us (4%)
  loops' own time  9.12 us (2%)
    all_gather x1, waiting for transfers between devices, per_device(): full_up = lax.all_gather(up_weight, 'blk', axis=0, tiled=True)  110 us
    reduce_scatter x1, waiting for transfers between devices, per_device(): lax.psum_scatter(partial_sum.astype(jnp.bfloat16), 'head', scatter_dimens...  46.9 us
    ppermute x14, starting transfers between devices, from_behind(): lax.ppermute(value, axis, [(source, source + steps) for source in range(i...  43.9 us
    dot_general x6, matrix products, key_values(): jnp.dot(carried_block, full_up, preferred_element_type=jnp.float32)  31.3 us
    dot_general x6, matrix products, update(): jnp.einsum('hqk,khv->hqv', weights.astype(jnp.bfloat16), expanded[:, :, D...  21.1 us
    dot_general x1, matrix products, per_device(): jnp.dot(outputs, out_weight, preferred_element_type=jnp.float32)  17.3 us
    ppermute x14, waiting for transfers between devices, from_behind(): lax.ppermute(value, axis, [(source, source + steps) for source in range(i...  14.5 us
    cond x33, local copies, waits for them, and re-layouts  14.1 us
  transfers between devices with their start and end apart: 16, of which 9 were waited for; matrix products, arithmetic and copies ran while one was open for 7% of the time, Pallas kernels for 0%

commit v1 on v0

v1 whole, which is shorter than its diff:
```python
import functools
import math

import jax
import jax.numpy as jnp
from jax import lax
from jax.experimental import pallas as pl
from jax.experimental.pallas import tpu as pltpu
from jax.sharding import PartitionSpec as P

DN = 128
DR = 64
DV = 128
QB = 96
NEG = -1e30
HPC = 4
PARTS = 4
MESH = pl.DeviceIdType.MESH


def ring_place(index, n):
    return jnp.where(index % 2 == 0, index // 2, n - 1 - index // 2)


def ring_index(place, n):
    place = lax.rem(place + 2 * n, n)
    return jnp.where(place < n // 2, 2 * place, 2 * (n - 1 - place) + 1)


def kernel(
    n, nh, mask_ref, q_ref, lat_ref, up_ref, ow_ref, out_ref,
    wfull, lat, wo, acc, scores, peak, qs, vals, mix, bias, heads_out,
    give1, take1, give2, take2,
    cw_send, cw_recv, cc_send, cc_recv,
    lcw_send, lcw_recv, lcc_send, lcc_recv, lp_send, lp_recv,
    wo_sem, r1_send, r1_recv, r2_send, r2_recv,
):
    tok = q_ref.shape[0]
    rows = up_ref.shape[0]
    nchunk, _, cw = wfull.shape
    half = n // 2
    kc = 2 * tok
    kvr = n * rows
    ocols = out_ref.shape[1]
    nchip = nh // 2
    my = lax.axis_index("blk")
    hd = lax.axis_index("head")
    place = ring_place(my, n)
    right = ring_index(place + 1, n)
    left = ring_index(place + n - 1, n)
    part = lax.rem(hd, PARTS)
    base = hd - part
    prow = tok // PARTS
    core = lax.rem(hd, 2)
    chip = hd // 2
    mate = chip * 2 + 1 - core
    scale = math.log2(math.e) / math.sqrt(DN + DR)

    barrier = pltpu.get_barrier_semaphore()
    for other in (left, right):
        pl.semaphore_signal(barrier, inc=1, device_id=(other, hd), device_id_type=MESH)
    for d in range(1, nh):
        pl.semaphore_signal(barrier, inc=1, device_id=(my, lax.rem(hd + d, nh)), device_id_type=MESH)
    pl.semaphore_wait(barrier, 2 + nh - 1)

    def wmsg(c, k, clockwise):
        origin = ring_index(place - (k - 1), n) if clockwise else ring_index(place + (k - 1), n)
        start, size = origin * rows, rows
        if k == half:
            size = rows // 2
            if not clockwise:
                start = start + size
        block = wfull.at[c, pl.ds(pl.multiple_of(start, 16), size), :]
        return pltpu.make_async_remote_copy(
            src_ref=block, dst_ref=block,
            send_sem=(cw_send if clockwise else cc_send).at[c, k - 1],
            recv_sem=(cw_recv if clockwise else cc_recv).at[c, k - 1],
            device_id=(right if clockwise else left, hd), device_id_type=MESH,
        )

    def wgot(c, k, clockwise):
        origin = ring_index(place - k, n) if clockwise else ring_index(place + k, n)
        start, size = origin * rows, rows
        if k == half:
            size = rows // 2
            if not clockwise:
                start = start + size
        block = wfull.at[c, pl.ds(pl.multiple_of(start, 16), size), :]
        return pltpu.make_async_remote_copy(
            src_ref=block, dst_ref=block,
            send_sem=(cw_send if clockwise else cc_send).at[c, k - 1],
            recv_sem=(cw_recv if clockwise else cc_recv).at[c, k - 1],
            device_id=(right if clockwise else left, hd), device_id_type=MESH,
        )

    def lmsg(k, clockwise, received):
        steps = k if received else k - 1
        origin = ring_index(place - steps, n) if clockwise else ring_index(place + steps, n)
        block = lat.at[origin, part]
        return pltpu.make_async_remote_copy(
            src_ref=block, dst_ref=block,
            send_sem=(lcw_send if clockwise else lcc_send).at[k - 1],
            recv_sem=(lcw_recv if clockwise else lcc_recv).at[k - 1],
            device_id=(right if clockwise else left, hd), device_id_type=MESH,
        )

    def lpeer(k, clockwise, d, received):
        origin = ring_index(place - k, n) if clockwise else ring_index(place + k, n)
        e = (k - 1) * 2 + (0 if clockwise else 1)
        owner = lax.rem(part + PARTS - d, PARTS) if received else part
        block = lat.at[origin, owner]
        return pltpu.make_async_remote_copy(
            src_ref=block, dst_ref=block,
            send_sem=lp_send.at[e, d - 1], recv_sem=lp_recv.at[e, d - 1],
            device_id=(my, base + lax.rem(part + d, PARTS)), device_id_type=MESH,
        )

    lat_hops = [(k, way) for k in range(1, half + 1) for way in (True, False) if way or k < half]

    lat[my] = lat_ref[...].reshape(PARTS, prow, lat_ref.shape[1])
    lmsg(1, True, False).start()
    lmsg(1, False, False).start()

    own_rows = pl.ds(pl.multiple_of(my * rows, 16), rows)

    def fill(c, _):
        wfull[c, own_rows, :] = up_ref[:, pl.ds(pl.multiple_of(c * cw, 128), cw)]
        return 0

    lax.fori_loop(0, nchunk, fill, 0)

    def wo_copy(c):
        slot = lax.rem(c, 2)
        return pltpu.make_async_copy(
            ow_ref.at[pl.ds(pl.multiple_of(c * (HPC * DV), 128), HPC * DV), :],
            wo.at[slot], wo_sem.at[slot],
        )

    nj = my // 2 + 1

    def send_group(t, k):
        c = t - (k - 1)

        @pl.when((c >= 0) & (c < nchunk))
        def _():
            if k > 1:
                wgot(c, k - 1, True).wait_recv()
            wmsg(c, k, True).start()
            if k > 1:
                wgot(c, k - 1, False).wait_recv()
            wmsg(c, k, False).start()

    def project(c, o):
        slot = lax.rem(c, 2)
        columns = pl.ds(pl.multiple_of(o * ocols, 128), ocols)
        return acc[o] + jnp.dot(
            heads_out[...], wo[slot, :, columns], preferred_element_type=jnp.float32
        )

    def phase_a(c):
        qc = q_ref[:, pl.ds(pl.multiple_of(c * (HPC * (DN + DR)), 128), HPC * (DN + DR))]
        pad = jnp.zeros((tok, 256 - DN - DR), qc.dtype)
        for h in range(HPC):
            qs[h] = jnp.concatenate([qc[:, h * (DN + DR) : (h + 1) * (DN + DR)], pad], axis=1)
            peak[h] = jnp.full((tok, 128), NEG, jnp.float32)
            mix[h] = jnp.zeros((tok, 256), jnp.float32)

        def step(j, _):
            block = lat[pl.ds(2 * j, 2)].reshape(kc, lat_ref.shape[1])
            rope = block[:, kvr:]
            kv = jnp.dot(
                block[:, :kvr], wfull[c], preferred_element_type=jnp.float32
            ).astype(jnp.bfloat16)
            for h in range(HPC):
                key = jnp.concatenate([kv[:, h * 256 : h * 256 + DN], rope], axis=1)
                vals[h, j] = kv[:, h * 256 + DN : (h + 1) * 256]
                s = lax.dot_general(
                    qs[h], key, (((1,), (1,)), ((), ())), preferred_element_type=jnp.float32
                )
                s = s * scale + bias[j]
                scores[h, j] = s
                top = peak[h]
                for g in range(kc // 128):
                    top = jnp.maximum(top, s[:, g * 128 : (g + 1) * 128])
                peak[h] = top
            return 0

        lax.fori_loop(0, nj, step, 0)

    def phase_b():
        for h in range(HPC):
            peak[h] = jnp.broadcast_to(jnp.max(peak[h], axis=1, keepdims=True), (tok, 128))
        ones = jnp.ones((kc, 128), jnp.bfloat16)

        def step(j, _):
            for h in range(HPC):
                top = peak[h]
                p = jnp.concatenate(
                    [
                        jnp.exp2(scores[h, j, :, g * 128 : (g + 1) * 128] - top).astype(jnp.bfloat16)
                        for g in range(kc // 128)
                    ],
                    axis=1,
                )
                v = jnp.concatenate([vals[h, j], ones], axis=1)
                mix[h] += jnp.dot(p, v, preferred_element_type=jnp.float32)
            return 0

        lax.fori_loop(0, nj, step, 0)
        for h in range(HPC):
            m = mix[h]
            heads_out[:, h * DV : (h + 1) * DV] = (m[:, :DV] / m[:, DV:]).astype(jnp.bfloat16)

    def tick(t, _):
        c = t - half
        live = c >= 0
        upper = list(range(half, 0, -1))
        first = upper[: max(1, half // 2)]
        second = upper[max(1, half // 2) :]
        for k in first:
            send_group(t, k)

        for k, way in lat_hops:
            @pl.when(t == k)
            def _(k=k, way=way):
                lmsg(k, way, True).wait_recv()
                if (k + 1, way) in lat_hops:
                    lmsg(k + 1, way, False).start()
                for d in range(1, PARTS):
                    lpeer(k, way, d, False).start()

        @pl.when(t == 0)
        def _():
            wo_copy(0).start()
            wo_copy(1).start()
            acc[...] = jnp.zeros_like(acc)
            lane = lax.broadcasted_iota(jnp.int32, (QB, kc), 1)
            row = lax.broadcasted_iota(jnp.int32, (QB, kc), 0)
            group = lane // QB
            for j in range(n // 2):
                for g in range(tok // QB):
                    bits = jnp.zeros((QB, kc), jnp.int32)
                    for b in range(kc // QB):
                        bit = mask_ref[my * (tok // QB) + g, j * (kc // QB) + b]
                        bits = jnp.where(group == b, bit, bits)
                    allowed = (bits == 1) & (lane + j * kc <= row + (my * tok + g * QB))
                    bias[j, g * QB : (g + 1) * QB, :] = jnp.where(allowed, 0.0, NEG)

        @pl.when(t == half)
        def _():
            for k, way in lat_hops:
                for d in range(1, PARTS):
                    lpeer(k, way, d, True).wait_recv()

        @pl.when(live)
        def _():
            wgot(c, half, True).wait_recv()
            wgot(c, half, False).wait_recv()
            phase_a(c)

        for k in second:
            send_group(t, k)

        @pl.when(live)
        def _():
            phase_b()
            wo_copy(c).wait()

        @pl.when(live & (c < nchunk - 1))
        def _():
            def one(o, _):
                acc[o] = project(c, o)
                return 0

            lax.fori_loop(0, nh, one, 0)

            @pl.when(c + 2 < nchunk)
            def _():
                wo_copy(c + 2).start()

        return 0

    lax.fori_loop(0, nchunk + half, tick, 0)

    last = nchunk - 1

    def stage1(i):
        return pltpu.make_async_remote_copy(
            src_ref=give1.at[i], dst_ref=take1.at[i], send_sem=r1_send.at[i],
            recv_sem=r1_recv.at[i], device_id=(my, mate), device_id_type=MESH,
        )

    def stage2(i):
        to = lax.rem(chip + i, nchip) * 2 + core
        return pltpu.make_async_remote_copy(
            src_ref=give2.at[i - 1], dst_ref=take2.at[i - 1], send_sem=r2_send.at[i - 1],
            recv_sem=r2_recv.at[i - 1], device_id=(my, to), device_id_type=MESH,
        )

    order = list(range(1, nchip)) + [0]
    for i in order:
        to = lax.rem(chip + i, nchip) * 2 + 1 - core
        give1[i] = project(last, to).astype(jnp.bfloat16)
        stage1(i).start()
    for i in order[:-1]:
        to = lax.rem(chip + i, nchip) * 2 + core
        mine = project(last, to)
        stage1(i).wait_recv()
        give2[i - 1] = (mine + take1[i].astype(jnp.float32)).astype(jnp.bfloat16)
        stage2(i).start()
    total = project(last, hd)
    stage1(0).wait_recv()
    total = total + take1[0].astype(jnp.float32)
    acc[0] = total
    for i in order[:-1]:
        stage2(i).wait_recv()
        acc[0] += take2[i - 1].astype(jnp.float32)
    out_ref[...] = acc[0].astype(jnp.bfloat16)

    def drain(c, _):
        for k in range(1, half + 1):
            wmsg(c, k, True).wait_send()
            wmsg(c, k, False).wait_send()
        return 0

    lax.fori_loop(0, nchunk, drain, 0)
    for k, way in lat_hops:
        lmsg(k, way, False).wait_send()
        for d in range(1, PARTS):
            lpeer(k, way, d, False).wait_send()
    for i in order:
        stage1(i).wait_send()
    for i in order[:-1]:
        stage2(i).wait_send()


def per_device(n, nh, query_heads, latent_cache, rope_keys, up_weight, out_weight, block_mask):
    tok = query_heads.shape[0]
    heads = out_weight.shape[0] // DV
    kvr = latent_cache.shape[1]
    rows = up_weight.shape[0]
    width = out_weight.shape[1]
    ocols = width // nh
    nchunk = heads // HPC
    half = n // 2
    kc = 2 * tok
    lw = kvr + 128
    latent = jnp.concatenate(
        [latent_cache, rope_keys, jnp.zeros((tok, 128 - DR), latent_cache.dtype)], axis=1
    )
    bf16, f32 = jnp.bfloat16, jnp.float32
    dma = pltpu.SemaphoreType.DMA
    nchip = nh // 2
    vmem = pl.BlockSpec(memory_space=pltpu.VMEM)
    return pl.pallas_call(
        functools.partial(kernel, n, nh),
        out_shape=jax.ShapeDtypeStruct((tok, ocols), bf16),
        in_specs=[
            pl.BlockSpec(memory_space=pltpu.SMEM), vmem, vmem, vmem,
            pl.BlockSpec(memory_space=pl.ANY),
        ],
        out_specs=vmem,
        scratch_shapes=[
            pltpu.VMEM((nchunk, kvr, HPC * 256), bf16),
            pltpu.VMEM((n, PARTS, tok // PARTS, lw), bf16),
            pltpu.VMEM((2, HPC * DV, width), bf16),
            pltpu.VMEM((nh, tok, ocols), f32),
            pltpu.VMEM((HPC, n // 2, tok, kc), f32),
            pltpu.VMEM((HPC, tok, 128), f32),
            pltpu.VMEM((HPC, tok, 256), bf16),
            pltpu.VMEM((HPC, n // 2, kc, DV), bf16),
            pltpu.VMEM((HPC, tok, 256), f32),
            pltpu.VMEM((n // 2, tok, kc), f32),
            pltpu.VMEM((tok, HPC * DV), bf16),
            pltpu.VMEM((nchip, tok, ocols), bf16),
            pltpu.VMEM((nchip, tok, ocols), bf16),
            pltpu.VMEM((nchip - 1, tok, ocols), bf16),
            pltpu.VMEM((nchip - 1, tok, ocols), bf16),
            dma((nchunk, half)), dma((nchunk, half)), dma((nchunk, half)), dma((nchunk, half)),
            dma((half,)), dma((half,)), dma((half,)), dma((half,)),
            dma((2 * half, PARTS - 1)), dma((2 * half, PARTS - 1)),
            dma((2,)), dma((nchip,)), dma((nchip,)), dma((nchip - 1,)), dma((nchip - 1,)),
        ],
        compiler_params=pltpu.CompilerParams(
            collective_id=0, has_side_effects=True, vmem_limit_bytes=60 * 1024 * 1024
        ),
    )(block_mask, query_heads, latent, up_weight, out_weight)


def solution(mesh):
    n, nh = mesh.shape["blk"], mesh.shape["head"]
    return jax.shard_map(
        functools.partial(per_device, n, nh),
        mesh=mesh,
        in_specs=(
            P("blk", "head"), P("blk", None), P("blk", None),
            P("blk", "head"), P("head", None), P(),
        ),
        out_specs=P("blk", "head"),
        check_vma=False,
    )
```

time: 401 us -> 130 us (0.32); the launches traced: 396 us -> 129 us
  waiting for transfers between devices: 171 us -> 0 us
  Pallas kernels: 0 us -> 125 us
  matrix products: 86.5 us -> 0 us
  starting transfers between devices: 44 us -> 0 us
  local copies, waits for them, and re-layouts: 38.5 us -> 2.79 us
  other arithmetic: 31.5 us -> 1.68 us
  between operations: 14.6 us -> 0.01 us
  loops' own time: 9.12 us -> 0 us
    pallas_call x0 -> x1, Pallas kernels: none -> 125 us  [per_device(): pl.pallas_call(functools.partial(kernel, n, nh), out_shape=jax.ShapeDtype...]
    all_gather x1 -> x0, waiting for transfers between devices: 110 us -> none  [per_device(): full_up = lax.all_gather(up_weight, 'blk', axis=0, tiled=True)]
    dot_general x25 -> x0, matrix products: 86.5 us -> none  [the longest x6 31.3 us: key_values(): jnp.dot(carried_block, full_up, preferred_element_type=jnp.float32)]
    reduce_scatter x1 -> x0, waiting for transfers between devices: 46.9 us -> none  [per_device(): lax.psum_scatter(partial_sum.astype(jnp.bfloat16), 'head', scatter_dimens...]
    ppermute x14 -> x0, starting transfers between devices: 43.9 us -> none  [from_behind(): lax.ppermute(value, axis, [(source, source + steps) for source in range(i...]
    ppermute x14 -> x0, waiting for transfers between devices: 14.5 us -> none  [from_behind(): lax.ppermute(value, axis, [(source, source + steps) for source in range(i...]
    cond x33 -> x0, local copies, waits for them, and re-layouts: 14.1 us -> none
    another operation x9 -> x0, loops' own time: 9.12 us -> none  [the longest x1 8.59 us: per_device(): lax.fori_loop(1, cycle_size, cycle_turn, (payload, status))]
  transfers between devices with their start and end apart: 16 -> 0, of which waited for: 9 -> 0; matrix products, arithmetic and copies ran while one was open for 7% -> 0% of each run, Pallas kernels for 0% -> 0%
where the time goes in v1:
time: 130 us; the launch traced here: 129 us
  Pallas kernels  125 us (96%)
  local copies, waits for them, and re-layouts  2.79 us (2%)
  other arithmetic  1.68 us (1%)
    pallas_call x1, Pallas kernels, per_device(): pl.pallas_call(functools.partial(kernel, n, nh), out_shape=jax.ShapeDtype...  125 us
    unnamed x2, local copies, waits for them, and re-layouts  2.7 us

profile of v1, /device:TPU:24, one launch (start us, length us, event | category | flops | bytes accessed | tf_op | source)
XLA Modules:
  0.0 129.5 jit_solution(16848625593982987210)
XLA Ops:
  0.0 0.1 pad.2.clone
  0.1 0.9 copy.7
  0.9 1.7 %maximum_maximum_fusion.lat_ref = bf16[192,640]{1,0:T(8,128)(2,1)} fusion(bf16[192,64]{1,0:T(8,128)(2,1)S(1)} %copy.7, bf16[192,512]{1,0:T(8,128)(2,1)} %param.7, bf16[640]{0:T(1024)(128)(2,1)S(1)} %pad.2.clone), kind=kLoop, calls=%fused_computation | loop fusion | flops 737280 | bytes 468224 | tf_op jit(solution)/shard_map/concatenate | solution.py:348
  2.6 125.0 %shard_map.64 = bf16[192,1280]{1,0:T(8,128)(2,1)} custom-call(s32[16,16]{1,0:T(8,128)} %mask_ref.1, bf16[192,6144]{1,0:T(8,128)(2,1)} %q_ref.1, bf16[192,640]{1,0:T(8,128)(2,1)} %maximum_maximum_fusion.lat_ref, bf16[64,8192]{1,0:T(8,128)(2,1)} %up_ref.1, bf16[4096,5120]{1,0:T(8,128)(2,1)} %ow_ref.1), custom_call_target="tpu_custom_call" | custom-call | tf_op jit(solution)/shard_map/pallas_call | solution.py:355
  127.6 1.8 %copy.9 = bf16[192,1280]{1,0:T(8,128)(2,1)} copy(bf16[192,1280]{1,0:T(8,128)(2,1)} %shard_map.64) | data formatting | bytes 983040
  (1 shorter events, 0.0 us)

commit v2 on v1

--- a/solution.py
+++ b/solution.py
@@ -13,7 +13,7 @@
 DV = 128
 QB = 96
 NEG = -1e30
-HPC = 4
+HPC = 2
 PARTS = 4
 MESH = pl.DeviceIdType.MESH
 
@@ -28,12 +28,13 @@
 
 
 def kernel(
-    n, nh, mask_ref, q_ref, lat_ref, up_ref, ow_ref, out_ref,
+    n, nh, mask_ref, q_hbm, lat_ref, rope_ref, up_ref, ow_ref, out_ref,
+    q_ref,
     wfull, lat, wo, acc, scores, peak, qs, vals, mix, bias, heads_out,
     give1, take1, give2, take2,
     cw_send, cw_recv, cc_send, cc_recv,
     lcw_send, lcw_recv, lcc_send, lcc_recv, lp_send, lp_recv,
-    wo_sem, r1_send, r1_recv, r2_send, r2_recv,
+    wo_sem, q_sem, r1_send, r1_recv, r2_send, r2_recv,
 ):
     tok = q_ref.shape[0]
     rows = up_ref.shape[0]
@@ -117,7 +118,10 @@
 
     lat_hops = [(k, way) for k in range(1, half + 1) for way in (True, False) if way or k < half]
 
-    lat[my] = lat_ref[...].reshape(PARTS, prow, lat_ref.shape[1])
+    joined = jnp.concatenate(
+        [lat_ref[...], rope_ref[...], jnp.zeros((tok, 128 - DR), lat_ref.dtype)], axis=1
+    )
+    lat[my] = joined.reshape(PARTS, prow, kvr + 128)
     lmsg(1, True, False).start()
     lmsg(1, False, False).start()
 
@@ -127,7 +131,12 @@
         wfull[c, own_rows, :] = up_ref[:, pl.ds(pl.multiple_of(c * cw, 128), cw)]
         return 0
 
-    lax.fori_loop(0, nchunk, fill, 0)
+    fill(0, 0)
+    wmsg(0, 1, True).start()
+    wmsg(0, 1, False).start()
+    lax.fori_loop(1, nchunk, fill, 0)
+    q_copy = pltpu.make_async_copy(q_hbm, q_ref, q_sem)
+    q_copy.start()
 
     def wo_copy(c):
         slot = lax.rem(c, 2)
@@ -166,7 +175,7 @@
             mix[h] = jnp.zeros((tok, 256), jnp.float32)
 
         def step(j, _):
-            block = lat[pl.ds(2 * j, 2)].reshape(kc, lat_ref.shape[1])
+            block = lat[pl.ds(2 * j, 2)].reshape(kc, kvr + 128)
             rope = block[:, kvr:]
             kv = jnp.dot(
                 block[:, :kvr], wfull[c], preferred_element_type=jnp.float32
@@ -248,6 +257,7 @@
 
         @pl.when(t == half)
         def _():
+            q_copy.wait()
             for k, way in lat_hops:
                 for d in range(1, PARTS):
                     lpeer(k, way, d, True).wait_recv()
@@ -259,7 +269,7 @@
             phase_a(c)
 
         for k in second:
-            send_group(t, k)
+            send_group(t + 1, k)
 
         @pl.when(live)
         def _():
@@ -345,9 +355,6 @@
     half = n // 2
     kc = 2 * tok
     lw = kvr + 128
-    latent = jnp.concatenate(
-        [latent_cache, rope_keys, jnp.zeros((tok, 128 - DR), latent_cache.dtype)], axis=1
-    )
     bf16, f32 = jnp.bfloat16, jnp.float32
     dma = pltpu.SemaphoreType.DMA
     nchip = nh // 2
@@ -356,11 +363,12 @@
         functools.partial(kernel, n, nh),
         out_shape=jax.ShapeDtypeStruct((tok, ocols), bf16),
         in_specs=[
-            pl.BlockSpec(memory_space=pltpu.SMEM), vmem, vmem, vmem,
-            pl.BlockSpec(memory_space=pl.ANY),
+            pl.BlockSpec(memory_space=pltpu.SMEM), pl.BlockSpec(memory_space=pl.ANY),
+            vmem, vmem, vmem, pl.BlockSpec(memory_space=pl.ANY),
         ],
         out_specs=vmem,
         scratch_shapes=[
+            pltpu.VMEM(query_heads.shape, bf16),
             pltpu.VMEM((nchunk, kvr, HPC * 256), bf16),
             pltpu.VMEM((n, PARTS, tok // PARTS, lw), bf16),
             pltpu.VMEM((2, HPC * DV, width), bf16),
@@ -379,12 +387,12 @@
             dma((nchunk, half)), dma((nchunk, half)), dma((nchunk, half)), dma((nchunk, half)),
             dma((half,)), dma((half,)), dma((half,)), dma((half,)),
             dma((2 * half, PARTS - 1)), dma((2 * half, PARTS - 1)),
-            dma((2,)), dma((nchip,)), dma((nchip,)), dma((nchip - 1,)), dma((nchip - 1,)),
+            dma((2,)), dma, dma((nchip,)), dma((nchip,)), dma((nchip - 1,)), dma((nchip - 1,)),
         ],
         compiler_params=pltpu.CompilerParams(
             collective_id=0, has_side_effects=True, vmem_limit_bytes=60 * 1024 * 1024
         ),
-    )(block_mask, query_heads, latent, up_weight, out_weight)
+    )(block_mask, query_heads, latent_cache, rope_keys, up_weight, out_weight)
 
 
 def solution(mesh):

time: 130 us -> 134 us (1.031)
  Pallas kernels: 125 us -> 131 us
  other arithmetic: 1.68 us -> 0 us
    pallas_call x1, Pallas kernels: 125 us -> 131 us  [per_device(): pl.pallas_call(functools.partial(kernel, n, nh), out_shape=jax.ShapeDtype...]
    concatenate x1 -> x0, other arithmetic: 1.68 us -> none  [per_device(): jnp.concatenate([latent_cache, rope_keys, jnp.zeros((tok, 128 - DR), late...]
where the time goes in v2:
time: 134 us
  Pallas kernels  131 us (98%)
  local copies, waits for them, and re-layouts  3.32 us (2%)
    pallas_call x1, Pallas kernels, per_device(): pl.pallas_call(functools.partial(kernel, n, nh), out_shape=jax.ShapeDtype...  131 us
    unnamed x2, local copies, waits for them, and re-layouts  3.32 us

profile of v2, /device:TPU:24, one launch (start us, length us, event | category | flops | bytes accessed | tf_op | source)
XLA Modules:
  0.0 133.9 jit_solution(5182890544509791457)
XLA Ops:
  0.0 1.5 %copy.7.rope_ref = bf16[192,64]{1,0:T(8,128)(2,1)} copy(bf16[192,64]{0,1:T(8,128)(2,1)} %param.8) | data formatting | bytes 49152 | tf_op args[2]
  1.5 130.5 %shard_map.64 = bf16[192,1280]{1,0:T(8,128)(2,1)} custom-call(s32[16,16]{1,0:T(8,128)} %mask_ref.1, bf16[192,6144]{1,0:T(8,128)(2,1)} %q_hbm.1, bf16[192,512]{1,0:T(8,128)(2,1)} %lat_ref.1, bf16[192,64]{1,0:T(8,128)(2,1)} %copy.7.rope_ref, bf16[64,8192]{1,0:T(8,128)(2,1)} %up_ref.1, bf16[4096,5120]{1,0:T(8,128)(2,1)} %ow_ref.1), custom_call_target="tpu_custom_call" | custom-call | tf_op jit(solution)/shard_map/pallas_call | solution.py:362
  132.0 1.8 %copy.9 = bf16[192,1280]{1,0:T(8,128)(2,1)} copy(bf16[192,1280]{1,0:T(8,128)(2,1)} %shard_map.64) | data formatting | bytes 983040

commit v3 on v2

--- a/solution.py
+++ b/solution.py
@@ -13,7 +13,9 @@
 DV = 128
 QB = 96
 NEG = -1e30
-HPC = 2
+HPC = 4
+HPM = 2
+SUB = HPC // HPM
 PARTS = 4
 MESH = pl.DeviceIdType.MESH
 
@@ -38,7 +40,8 @@
 ):
     tok = q_ref.shape[0]
     rows = up_ref.shape[0]
-    nchunk, _, cw = wfull.shape
+    nsub, _, cw = wfull.shape
+    nchunk = nsub // SUB
     half = n // 2
     kc = 2 * tok
     kvr = n * rows
@@ -134,7 +137,7 @@
     fill(0, 0)
     wmsg(0, 1, True).start()
     wmsg(0, 1, False).start()
-    lax.fori_loop(1, nchunk, fill, 0)
+    lax.fori_loop(1, nsub, fill, 0)
     q_copy = pltpu.make_async_copy(q_hbm, q_ref, q_sem)
     q_copy.start()
 
@@ -150,7 +153,7 @@
     def send_group(t, k):
         c = t - (k - 1)
 
-        @pl.when((c >= 0) & (c < nchunk))
+        @pl.when((c >= 0) & (c < nsub))
         def _():
             if k > 1:
                 wgot(c, k - 1, True).wait_recv()
@@ -177,12 +180,16 @@
         def step(j, _):
             block = lat[pl.ds(2 * j, 2)].reshape(kc, kvr + 128)
             rope = block[:, kvr:]
-            kv = jnp.dot(
-                block[:, :kvr], wfull[c], preferred_element_type=jnp.float32
-            ).astype(jnp.bfloat16)
+            kvs = [
+                jnp.dot(
+                    block[:, :kvr], wfull[c * SUB + i], preferred_element_type=jnp.float32
+                ).astype(jnp.bfloat16)
+                for i in range(SUB)
+            ]
             for h in range(HPC):
-                key = jnp.concatenate([kv[:, h * 256 : h * 256 + DN], rope], axis=1)
-                vals[h, j] = kv[:, h * 256 + DN : (h + 1) * 256]
+                kv, at = kvs[h // HPM], (h % HPM) * 256
+                key = jnp.concatenate([kv[:, at : at + DN], rope], axis=1)
+                vals[h, j] = kv[:, at + DN : at + 256]
                 s = lax.dot_general(
                     qs[h], key, (((1,), (1,)), ((), ())), preferred_element_type=jnp.float32
                 )
@@ -221,13 +228,10 @@
             heads_out[:, h * DV : (h + 1) * DV] = (m[:, :DV] / m[:, DV:]).astype(jnp.bfloat16)
 
     def tick(t, _):
-        c = t - half
-        live = c >= 0
-        upper = list(range(half, 0, -1))
-        first = upper[: max(1, half // 2)]
-        second = upper[max(1, half // 2) :]
-        for k in first:
-            send_group(t, k)
+        u = t - half - 1
+        c = u // SUB
+        for k in range(half, 0, -1):
+            send_group(t if k > half // 2 else t + 1, k)
 
         for k, way in lat_hops:
             @pl.when(t == k)
@@ -255,28 +259,28 @@
                     allowed = (bits == 1) & (lane + j * kc <= row + (my * tok + g * QB))
                     bias[j, g * QB : (g + 1) * QB, :] = jnp.where(allowed, 0.0, NEG)
 
-        @pl.when(t == half)
+        @pl.when(t == half + 1)
         def _():
             q_copy.wait()
             for k, way in lat_hops:
                 for d in range(1, PARTS):
                     lpeer(k, way, d, True).wait_recv()
 
-        @pl.when(live)
-        def _():
-            wgot(c, half, True).wait_recv()
-            wgot(c, half, False).wait_recv()
+        @pl.when((u >= 0) & (lax.rem(u, SUB) == 0))
+        def _():
+            for i in range(SUB):
+                wgot(c * SUB + i, half, True).wait_recv()
+                wgot(c * SUB + i, half, False).wait_recv()
             phase_a(c)
 
-        for k in second:
-            send_group(t + 1, k)
-
-        @pl.when(live)
+        done = (u >= 0) & (lax.rem(u, SUB) == SUB - 1)
+
+        @pl.when(done)
         def _():
             phase_b()
             wo_copy(c).wait()
 
-        @pl.when(live & (c < nchunk - 1))
+        @pl.when(done & (c < nchunk - 1))
         def _():
             def one(o, _):
                 acc[o] = project(c, o)
@@ -290,7 +294,7 @@
 
         return 0
 
-    lax.fori_loop(0, nchunk + half, tick, 0)
+    lax.fori_loop(0, nsub + half + 1, tick, 0)
 
     last = nchunk - 1
 
@@ -333,7 +337,7 @@
             wmsg(c, k, False).wait_send()
         return 0
 
-    lax.fori_loop(0, nchunk, drain, 0)
+    lax.fori_loop(0, nsub, drain, 0)
     for k, way in lat_hops:
         lmsg(k, way, False).wait_send()
         for d in range(1, PARTS):
@@ -351,7 +355,7 @@
     rows = up_weight.shape[0]
     width = out_weight.shape[1]
     ocols = width // nh
-    nchunk = heads // HPC
+    nsub = heads // HPM
     half = n // 2
     kc = 2 * tok
     lw = kvr + 128
@@ -369,7 +373,7 @@
         out_specs=vmem,
         scratch_shapes=[
             pltpu.VMEM(query_heads.shape, bf16),
-            pltpu.VMEM((nchunk, kvr, HPC * 256), bf16),
+            pltpu.VMEM((nsub, kvr, HPM * 256), bf16),
             pltpu.VMEM((n, PARTS, tok // PARTS, lw), bf16),
             pltpu.VMEM((2, HPC * DV, width), bf16),
             pltpu.VMEM((nh, tok, ocols), f32),
@@ -384,7 +388,7 @@
             pltpu.VMEM((nchip, tok, ocols), bf16),
             pltpu.VMEM((nchip - 1, tok, ocols), bf16),
             pltpu.VMEM((nchip - 1, tok, ocols), bf16),
-            dma((nchunk, half)), dma((nchunk, half)), dma((nchunk, half)), dma((nchunk, half)),
+            dma((nsub, half)), dma((nsub, half)), dma((nsub, half)), dma((nsub, half)),
             dma((half,)), dma((half,)), dma((half,)), dma((half,)),
             dma((2 * half, PARTS - 1)), dma((2 * half, PARTS - 1)),
             dma((2,)), dma, dma((nchip,)), dma((nchip,)), dma((nchip - 1,)), dma((nchip - 1,)),

time: 134 us -> 131 us (0.978); the launches traced: 134 us -> 130 us
  Pallas kernels: 131 us -> 126 us
    pallas_call x1, Pallas kernels: 131 us -> 126 us  [per_device(): pl.pallas_call(functools.partial(kernel, n, nh), out_shape=jax.ShapeDtype...]
where the time goes in v3:
time: 131 us; the launch traced here: 130 us
  Pallas kernels  126 us (96%)
  local copies, waits for them, and re-layouts  3.32 us (3%)
    pallas_call x1, Pallas kernels, per_device(): pl.pallas_call(functools.partial(kernel, n, nh), out_shape=jax.ShapeDtype...  126 us
    unnamed x2, local copies, waits for them, and re-layouts  3.32 us

profile of v3, /device:TPU:24, one launch (start us, length us, event | category | flops | bytes accessed | tf_op | source)
XLA Modules:
  0.0 129.5 jit_solution(15414532276817402088)
XLA Ops:
  0.0 1.5 %copy.7.rope_ref = bf16[192,64]{1,0:T(8,128)(2,1)} copy(bf16[192,64]{0,1:T(8,128)(2,1)} %param.8) | data formatting | bytes 49152 | tf_op args[2]
  1.5 126.2 %shard_map.64 = bf16[192,1280]{1,0:T(8,128)(2,1)} custom-call(s32[16,16]{1,0:T(8,128)} %mask_ref.1, bf16[192,6144]{1,0:T(8,128)(2,1)} %q_hbm.1, bf16[192,512]{1,0:T(8,128)(2,1)} %lat_ref.1, bf16[192,64]{1,0:T(8,128)(2,1)} %copy.7.rope_ref, bf16[64,8192]{1,0:T(8,128)(2,1)} %up_ref.1, bf16[4096,5120]{1,0:T(8,128)(2,1)} %ow_ref.1), custom_call_target="tpu_custom_call" | custom-call | tf_op jit(solution)/shard_map/pallas_call | solution.py:366
  127.7 1.8 %copy.9 = bf16[192,1280]{1,0:T(8,128)(2,1)} copy(bf16[192,1280]{1,0:T(8,128)(2,1)} %shard_map.64) | data formatting | bytes 983040

commit v4 on v2

--- a/solution.py
+++ b/solution.py
@@ -13,7 +13,7 @@
 DV = 128
 QB = 96
 NEG = -1e30
-HPC = 2
+HPC = 4
 PARTS = 4
 MESH = pl.DeviceIdType.MESH
 
@@ -131,10 +131,7 @@
         wfull[c, own_rows, :] = up_ref[:, pl.ds(pl.multiple_of(c * cw, 128), cw)]
         return 0
 
-    fill(0, 0)
-    wmsg(0, 1, True).start()
-    wmsg(0, 1, False).start()
-    lax.fori_loop(1, nchunk, fill, 0)
+    lax.fori_loop(0, nchunk, fill, 0)
     q_copy = pltpu.make_async_copy(q_hbm, q_ref, q_sem)
     q_copy.start()
 
@@ -269,7 +266,7 @@
             phase_a(c)
 
         for k in second:
-            send_group(t + 1, k)
+            send_group(t, k)
 
         @pl.when(live)
         def _():

time: 134 us -> 128 us (0.955)
  Pallas kernels: 131 us -> 124 us
    pallas_call x1, Pallas kernels: 131 us -> 124 us  [per_device(): pl.pallas_call(functools.partial(kernel, n, nh), out_shape=jax.ShapeDtype...]
where the time goes in v4:
time: 128 us
  Pallas kernels  124 us (97%)
  local copies, waits for them, and re-layouts  3.32 us (3%)
    pallas_call x1, Pallas kernels, per_device(): pl.pallas_call(functools.partial(kernel, n, nh), out_shape=jax.ShapeDtype...  124 us
    unnamed x2, local copies, waits for them, and re-layouts  3.32 us

profile of v4, /device:TPU:24, one launch (start us, length us, event | category | flops | bytes accessed | tf_op | source)
XLA Modules:
  0.0 127.6 jit_solution(10812210194114994027)
XLA Ops:
  0.0 1.5 %copy.7.rope_ref = bf16[192,64]{1,0:T(8,128)(2,1)} copy(bf16[192,64]{0,1:T(8,128)(2,1)} %param.8) | data formatting | bytes 49152 | tf_op args[2]
  1.5 124.3 %shard_map.64 = bf16[192,1280]{1,0:T(8,128)(2,1)} custom-call(s32[16,16]{1,0:T(8,128)} %mask_ref.1, bf16[192,6144]{1,0:T(8,128)(2,1)} %q_hbm.1, bf16[192,512]{1,0:T(8,128)(2,1)} %lat_ref.1, bf16[192,64]{1,0:T(8,128)(2,1)} %copy.7.rope_ref, bf16[64,8192]{1,0:T(8,128)(2,1)} %up_ref.1, bf16[4096,5120]{1,0:T(8,128)(2,1)} %ow_ref.1), custom_call_target="tpu_custom_call" | custom-call | tf_op jit(solution)/shard_map/pallas_call | solution.py:359
  125.8 1.8 %copy.9 = bf16[192,1280]{1,0:T(8,128)(2,1)} copy(bf16[192,1280]{1,0:T(8,128)(2,1)} %shard_map.64) | data formatting | bytes 983040
